TPU v7x, 256 devices: a whole 4x4x8 slice. The times are simulated.
256 devices in a mesh: dp: 16 (over x_hi, z), tensor: 16 (over x_lo, y, core).
Axes of the slice: x: 4 (x_hi: 2, x_lo: 2; x = x_hi * 2 + x_lo), y: 4, z: 8, core: 2. Of those that a mesh axis runs over, the one named last changes fastest.
Arguments:
- final_layer_states: bfloat16 [32768, 8192], P('dp', 'tensor'), may hold values from -64 to 64
- entry_rms_multiplier: float32 [8192], replicated, may hold values from 0.25 to 1.75
- group_sharpness: float32 [64], replicated, may hold values from 0.1 to 1
- ancestor_ids: int32 [32768], P('dp'), may hold values from 0 to 62, as said below
- proposal_matrix: bfloat16 [8192, 4096], P('dp', 'tensor'), may hold values from -0.0625 to 0.0625
- future_vectors: bfloat16 [32768, 4096], P('dp', 'tensor'), may hold values from -6 to 6
Outputs:
- predicted: bfloat16 [32768, 4096], P('dp', 'tensor')
- weight_grad: float32 [8192, 4096], P('dp', 'tensor')
Inputs may be any that keep to these rules, and one draw needn't show every extreme that they name: `ancestor_ids`: within each aligned block of 64 tokens, a token's entry is the in-block index of its parent, smaller than its own in-block index; the block's first token has 0, and its last token's parent is the one just before it.
All inputs are finite; a program needn't handle non-finite values.
Results may differ from a plain program's by a relative error of at most 0.012.
Values may be sent and summed in bfloat16 or wider, within the bound.
No kernel may reach another device: no remote copies, remote signals or barrier semaphores. Data moves between devices by JAX's collectives and lax.ppermute only.
A program may use at most 128 MiB of HBM per device.

v0:
```python
import math

import jax
import jax.numpy as jnp
from jax import lax
from jax.sharding import PartitionSpec as P

PER_GROUP_DEPTH = 128
BLOCK = 64


def branching_query_mixer(rescaled_entry, ancestor_ids, group_sharpness):
    rows, width = rescaled_entry.shape
    blocks = rows // BLOCK
    heads_here = width // PER_GROUP_DEPTH
    index = jnp.arange(BLOCK, dtype=jnp.int32)
    grouped = ancestor_ids.reshape(blocks, BLOCK)
    link = ((grouped[:, :, None] == index[None, None, :]) & (index[None, :, None] > 0)).astype(
        jnp.float32
    )
    reach = link + jnp.eye(BLOCK, dtype=jnp.float32)[None]
    for sweep in range(6):
        reach = jnp.minimum(
            jnp.einsum("bts,bsu->btu", reach, reach, precision=lax.Precision.HIGHEST), 1.0
        )
    feats = rescaled_entry.reshape(blocks, BLOCK, heads_here, PER_GROUP_DEPTH)
    softmax_multiplier = group_sharpness / math.sqrt(PER_GROUP_DEPTH)
    scores = (
        jnp.einsum("bthd,bshd->bhts", feats, feats, preferred_element_type=jnp.float32)
        * softmax_multiplier[None, :, None, None]
    )
    scores = jnp.where(reach[:, None] > 0, scores, -1e30)
    top = jnp.max(scores, axis=-1, keepdims=True)
    expd = jnp.exp(scores - top)
    probs = (expd / jnp.sum(expd, axis=-1, keepdims=True)).astype(jnp.bfloat16)
    blended_result = jnp.einsum("bhts,bshd->bthd", probs, feats, preferred_element_type=jnp.float32)
    return blended_result.astype(jnp.bfloat16).reshape(rows, width)


def body(
    final_layer_states,
    entry_rms_multiplier,
    group_sharpness,
    ancestor_ids,
    proposal_matrix,
    future_vectors,
):
    tok_rows, col_count = final_layer_states.shape
    tensor_index = lax.axis_index("tensor")
    full_weight = lax.all_gather(proposal_matrix, "dp", axis=0, tiled=True)
    panel = lax.all_to_all(final_layer_states, "tensor", split_axis=0, concat_axis=1, tiled=True)
    row_count = panel.shape[0]
    wide_rows = panel.astype(jnp.float32)
    mean_sq = jnp.mean(wide_rows * wide_rows, axis=1, keepdims=True)
    rescaled_entry = (
        wide_rows * lax.rsqrt(mean_sq + 1e-05) * entry_rms_multiplier[None, :]
    ).astype(jnp.bfloat16)
    shard_ancestor_ids = lax.dynamic_slice_in_dim(ancestor_ids, tensor_index * row_count, row_count)
    blended_result = branching_query_mixer(rescaled_entry, shard_ancestor_ids, group_sharpness)
    piece = lax.all_gather(blended_result, "tensor", axis=0, tiled=True)
    result = jnp.dot(piece, full_weight, preferred_element_type=jnp.float32)
    targets = future_vectors.astype(jnp.float32)
    residual_grad = jnp.clip(result - targets, -1.0, 1.0).astype(jnp.bfloat16)
    partial_value = lax.dot_general(
        piece, residual_grad, (((0,), (0,)), ((), ())), preferred_element_type=jnp.float32
    )
    projected = result
    partial_value, projected = (partial_value, projected)
    summed = lax.psum_scatter(
        partial_value.astype(jnp.bfloat16), "dp", scatter_dimension=0, tiled=True
    ).astype(jnp.float32)
    weight_grad = summed / math.sqrt(tok_rows * lax.axis_size("dp"))
    return (projected.astype(jnp.bfloat16), weight_grad)


def solution(mesh):
    return jax.shard_map(
        body,
        mesh=mesh,
        in_specs=(P("dp", "tensor"), P(), P(), P("dp"), P("dp", "tensor"), P("dp", "tensor")),
        out_specs=(P("dp", "tensor"), P("dp", "tensor")),
        check_vma=False,
    )
```

profile of v0, /device:TPU:8, one launch (start us, length us, event | category | flops | bytes accessed | tf_op | source)
XLA Modules:
  0.0 539.1 jit_solution(4082746968920472110)
XLA Ops:
  7.2 0.0 copy-start.2
  7.2 0.0 all-gather.5.cloned.1.call-start
  7.2 0.7 all-gather.5.cloned.1.call-update
  7.9 5.9 %all-to-all-start = ((bf16[16,128,512]{2,1,0:T(8,128)(2,1)}), bf16[16,128,512]{2,1,0:T(8,128)(2,1)S(1)}, u32[]{:S(2)}, u32[]{:S(2)}) async-start(bf16[16,128,512]{2,1,0:T(8,128)(2,1)} %bitcast.26), calls=%async_computation | async-start | bytes 4194304 | tf_op jit(solution)/shard_map/all_to_all | solution.py:51
  13.8 0.0 all-gather.3.cloned.1.call-start
  13.8 0.8 dynamic_slice.3
  14.6 0.1 eq.22
  14.7 0.3 convolution_minimum_fusion.5
  15.0 0.2 convolution_minimum_fusion.4
  15.2 0.2 convolution_minimum_fusion.3
  15.4 0.2 convolution_minimum_fusion.2
  15.6 0.2 convolution_minimum_fusion.1
  15.8 0.2 fusion.11
  16.0 0.1 copy.18
  16.1 0.0 copy-done.2
  16.1 27.4 %all-to-all-done = bf16[16,128,512]{2,1,0:T(8,128)(2,1)S(1)} async-done(((bf16[16,128,512]{2,1,0:T(8,128)(2,1)}), bf16[16,128,512]{2,1,0:T(8,128)(2,1)S(1)}, u32[]{:S(2)}, u32[]{:S(2)}) %all-to-all-start) | async-done | bytes 2097184 | tf_op jit(solution)/shard_map/all_to_all | solution.py:51
  43.5 0.5 fusion.1
  44.0 0.1 rsqrt.12
  44.1 0.6 convert_bitcast_fusion
  44.6 4.4 copy.17
  49.0 0.0 copy-start
  49.0 4.8 reshape.59
  53.8 0.0 copy-done
  53.8 2.7 multiply_convert_fusion
  56.5 2.5 fusion.8
  59.0 1.7 fusion.25
  60.7 2.5 convert_bitcast_fusion.1
  63.2 1.4 copy.23
  64.6 3.1 copy.31
  67.7 0.0 all-gather.3.cloned.1.call-update
  67.7 0.0 copy-start.1
  67.7 0.0 reduce-scatter.2.cloned.1.call-start
  67.8 47.4 %all-gather.5.cloned.1.call-done = bf16[8192,256]{1,0:T(8,128)(2,1)} async-done(((bf16[512,256]{1,0:T(8,128)(2,1)}), bf16[8192,256]{1,0:T(8,128)(2,1)}) %all-gather.5.cloned.1.call-update) | async-done | bytes 4194320 | tf_op jit(solution)/shard_map/all_gather | solution.py:50
  115.1 171.5 %all-gather.3.cloned.1.call-done = bf16[2048,8192]{1,0:T(8,128)(2,1)} async-done(((bf16[128,8192]{1,0:T(8,128)(2,1)}), bf16[2048,8192]{1,0:T(8,128)(2,1)}) %all-gather.3.cloned.1.call-update) | async-done | bytes 33554448 | tf_op jit(solution)/shard_map/all_gather | solution.py:60
  286.7 17.0 %fusion.26 = (bf16[2048,256]{1,0:T(8,128)(2,1)}, f32[2048,256]{1,0:T(8,128)S(1)}) fusion(bf16[2048,8192]{1,0:T(8,128)(2,1)} %all-gather.3.cloned.1.call-done, bf16[8192,256]{1,0:T(8,128)(2,1)} %all-gather.5.cloned.1.call-done), kind=kOutput, calls=%fused_computation.47 | convolution fusion | flops 8590458880 | bytes 40894464 | tf_op jit(solution)/shard_map/dot_general | solution.py:61
  303.7 0.0 copy-done.1
  303.7 17.3 %convolution_convert_fusion = bf16[8192,256]{1,0:T(8,128)(2,1)} fusion(bf16[2048,8192]{1,0:T(8,128)(2,1)} %all-gather.3.cloned.1.call-done, f32[2048,256]{1,0:T(8,128)S(1)} %get-tuple-element.5, bf16[2048,256]{1,0:T(8,128)(2,1)S(1)} %copy-done.1), kind=kOutput, calls=%fused_computation.1 | convolution fusion | flops 8594128896 | bytes 40894464 | tf_op jit(solution)/shard_map/dot_general | solution.py:64
  321.0 0.0 reduce-scatter.2.cloned.1.call-update
  321.0 209.7 %reduce-scatter.2.cloned.1.call-done = bf16[512,256]{1,0:T(8,128)(2,1)} async-done(((bf16[8192,256]{1,0:T(8,128)(2,1)}), bf16[512,256]{1,0:T(8,128)(2,1)}) %reduce-scatter.2.cloned.1.call-update) | async-done | bytes 262160 | tf_op jit(solution)/shard_map/reduce_scatter | solution.py:69
  530.7 1.8 convert_multiply_fusion.1
  (4 shorter events, 0.0 us)
Async XLA Ops:
  7.2 8.9 %copy-start.2 = (f32[64]{0:T(128)S(1)}, f32[64]{0:T(128)}, u32[]{:S(2)}) copy-start(f32[64]{0:T(128)} %param.8) | copy-start | bytes 772
  7.2 108.0 %all-gather.5.cloned.1.call-start = ((), (), s32[]{:S(2)}) async-start(), calls=%async_computation.3 | async-start | bytes 4456448 | tf_op jit(solution)/shard_map/all_gather | solution.py:50
  7.9 35.6 %all-to-all-start = ((bf16[16,128,512]{2,1,0:T(8,128)(2,1)}), bf16[16,128,512]{2,1,0:T(8,128)(2,1)S(1)}, u32[]{:S(2)}, u32[]{:S(2)}) async-start(bf16[16,128,512]{2,1,0:T(8,128)(2,1)} %bitcast.26), calls=%async_computation | async-start | bytes 4194304 | tf_op jit(solution)/shard_map/all_to_all | solution.py:51
  13.8 272.9 %all-gather.3.cloned.1.call-start = ((), (), s32[]{:S(2)}) async-start(), calls=%async_computation.2 | async-start | bytes 35651584 | tf_op jit(solution)/shard_map/all_gather | solution.py:60
  49.0 4.8 copy-start
  67.7 236.0 %copy-start.1 = (bf16[2048,256]{1,0:T(8,128)(2,1)S(1)}, bf16[2048,256]{1,0:T(8,128)(2,1)}, u32[]{:S(2)}) copy-start(bf16[2048,256]{1,0:T(8,128)(2,1)} %param.11) | copy-start | bytes 3145732
  67.7 463.0 %reduce-scatter.2.cloned.1.call-start = ((), (), s32[]{:S(2)}) async-start(), calls=%async_computation.4 | async-start | bytes 4456448 | tf_op jit(solution)/shard_map/reduce_scatter | solution.py:69
Sparse Core Ops, SparseCore 0:
  10.6 104.4 all-gather.4
  117.0 169.6 all-gather.2
  321.2 209.5 reduce-scatter.1
where the time goes:
time: 539 us
  waiting for transfers between devices  457 us (85%)
  matrix products  40.5 us (8%)
  local copies, waits for them, and re-layouts  14.7 us (3%)
  between operations  13.9 us (3%)
  other arithmetic  7.28 us (1%)
  starting transfers between devices  5.99 us (1%)
    reduce_scatter x1, waiting for transfers between devices, body(): lax.psum_scatter(partial_value.astype(jnp.bfloat16), 'dp', scatter_dimens...  210 us
    all_gather x1, waiting for transfers between devices, body(): piece = lax.all_gather(blended_result, 'tensor', axis=0, tiled=True)  172 us
    all_gather x1, waiting for transfers between devices, body(): full_weight = lax.all_gather(proposal_matrix, 'dp', axis=0, tiled=True)  47.4 us
    all_to_all x1, waiting for transfers between devices, body(): lax.all_to_all(final_layer_states, 'tensor', split_axis=0, concat_axis=1,...  27.4 us
    dot_general x1, matrix products, body(): lax.dot_general(piece, residual_grad, (((0,), (0,)), ((), ())), preferred...  17.3 us
    dot_general x1, matrix products, body(): result = jnp.dot(piece, full_weight, preferred_element_type=jnp.float32)  17 us
  transfers between devices with their start and end apart: 4, of which 4 were waited for; matrix products, arithmetic and copies ran while one was open for 5% of the time, Pallas kernels for 0%

commit v1 on v0

v1 whole, which is shorter than its diff:
```python
import functools
import math

import jax
import jax.numpy as jnp
from jax import lax
from jax.experimental import pallas as pl
from jax.experimental.pallas import tpu as pltpu
from jax.sharding import Mesh
from jax.sharding import PartitionSpec as P

HEAD = 128
BLOCK = 64
GROUP = 128
EPS = 1e-05
CHUNKS = (2048,)
BF16 = jnp.bfloat16
F32 = jnp.float32

GATHER_A = ((0, 2), (1, 0), (2, 3), (3, 1))
GATHER_B = ((1, 2), (2, 1))
SCATTER_A = tuple((dst, src) for src, dst in GATHER_A)
SCATTER_B = GATHER_B


def ring(n, step):
    return [(i, (i + step) % n) for i in range(n)]


def params(mib=48):
    return pltpu.CompilerParams(vmem_limit_bytes=mib * 1024 * 1024)


def reach_kernel(ids_ref, bias_ref):
    groups = ids_ref.shape[0]
    row = lax.broadcasted_iota(jnp.int32, (GROUP, GROUP), 0)
    col = lax.broadcasted_iota(jnp.int32, (GROUP, GROUP), 1)
    base = jnp.where(col >= BLOCK, BLOCK, 0)
    inner = (col != 0) & (col != BLOCK)
    eye = row == col
    reach = []
    for g in range(groups):
        parent = ids_ref[g : g + 1, :] + base
        hit = ((parent == row) & inner) | eye
        reach.append(jnp.where(hit, 1.0, 0.0).astype(BF16))
    for sweep in range(6):
        reach = [
            jnp.minimum(jnp.dot(r, r, preferred_element_type=F32), 1.0).astype(BF16) for r in reach
        ]
    for g in range(groups):
        bias = jnp.where(reach[g].astype(F32) > 0.0, 0.0, -1e30)
        bias_ref[g * GROUP : (g + 1) * GROUP, :] = bias.T


def reach_bias(ids):
    groups = ids.shape[0]
    return pl.pallas_call(
        reach_kernel,
        out_shape=jax.ShapeDtypeStruct((groups * GROUP, GROUP), F32),
        compiler_params=params(16),
        cost_estimate=pl.CostEstimate(
            flops=groups * 6 * 2 * GROUP**3, bytes_accessed=groups * GROUP * GROUP * 4, transcendentals=0
        ),
        name="reach",
    )(ids)


def attention_kernel(width, x_ref, sq_ref, bias_ref, gain_ref, sharp_ref, out_ref):
    groups = x_ref.shape[0] // GROUP
    heads = x_ref.shape[1] // HEAD
    row = lax.broadcasted_iota(jnp.int32, (GROUP, GROUP), 0)
    col = lax.broadcasted_iota(jnp.int32, (GROUP, GROUP), 1)
    eye = row == col
    gain = gain_ref[...]
    for g in range(groups):
        rows = slice(g * GROUP, (g + 1) * GROUP)
        scale = lax.rsqrt(sq_ref[0, g : g + 1, :] * (1.0 / width) + EPS)
        scale = jnp.sum(jnp.where(eye, scale, 0.0), axis=1, keepdims=True)
        normed = (x_ref[rows, :].astype(F32) * scale * gain).astype(BF16)
        bias = bias_ref[rows, :]
        for h in range(heads):
            cols = slice(h * HEAD, (h + 1) * HEAD)
            feats = normed[:, cols]
            scores = lax.dot_general(
                feats, feats, (((1,), (1,)), ((), ())), preferred_element_type=F32
            )
            scores = scores * (sharp_ref[0, h] * (1.0 / math.sqrt(HEAD))) + bias
            top = jnp.max(scores, axis=1, keepdims=True)
            expd = jnp.exp(scores - top)
            probs = (expd / jnp.sum(expd, axis=1, keepdims=True)).astype(BF16)
            mixed = jnp.dot(probs, feats, preferred_element_type=F32)
            out_ref[rows, cols] = mixed.astype(BF16)


def attention(states, squares, bias, gain, sharp, width, start, rows):
    cols = states.shape[1]
    tile = min(rows, 256)
    first = start // tile
    sub = tile // GROUP
    return pl.pallas_call(
        functools.partial(attention_kernel, width),
        grid=(rows // tile,),
        in_specs=[
            pl.BlockSpec((tile, cols), lambda i: (first + i, 0)),
            pl.BlockSpec((1, sub, GROUP), lambda i: (first + i, 0, 0)),
            pl.BlockSpec((tile, GROUP), lambda i: (first + i, 0)),
            pl.BlockSpec((1, cols), lambda i: (0, 0)),
            pl.BlockSpec(memory_space=pltpu.SMEM),
        ],
        out_specs=pl.BlockSpec((tile, cols), lambda i: (i, 0)),
        out_shape=jax.ShapeDtypeStruct((rows, cols), BF16),
        compiler_params=params(16),
        cost_estimate=pl.CostEstimate(
            flops=rows * GROUP * cols * 16, bytes_accessed=rows * cols * 4, transcendentals=rows * GROUP * 4
        ),
        name="attention",
    )(states, squares.reshape(-1, sub, GROUP), bias, gain, sharp)


def forward_kernel(pos_ref, mixed_ref, keep_w_ref, send_w_ref, keep_ref, send_ref):
    blocks = mixed_ref.shape[0]
    mixed = jnp.concatenate([mixed_ref[b] for b in range(blocks)], axis=1)
    depth = mixed.shape[1]
    keep_ref[...] = jnp.dot(
        mixed, keep_w_ref[...].reshape(depth, -1), preferred_element_type=F32
    )
    send_ref[...] = jnp.dot(
        mixed, send_w_ref[...].reshape(depth, -1), preferred_element_type=F32
    ).astype(BF16)


def forward(pos, mixed, weight):
    blocks, rows, depth = mixed.shape
    cols = weight.shape[3]
    tile = min(rows, 256)
    grid_spec = pltpu.PrefetchScalarGridSpec(
        num_scalar_prefetch=1,
        grid=(rows // tile,),
        in_specs=[
            pl.BlockSpec((blocks, tile, depth), lambda i, pos: (0, i, 0)),
            pl.BlockSpec((blocks, None, depth, cols), lambda i, pos: (0, pos[0], 0, 0)),
            pl.BlockSpec((blocks, None, depth, cols), lambda i, pos: (0, 1 - pos[0], 0, 0)),
        ],
        out_specs=[
            pl.BlockSpec((tile, cols), lambda i, pos: (i, 0)),
            pl.BlockSpec((tile, cols), lambda i, pos: (i, 0)),
        ],
    )
    return pl.pallas_call(
        forward_kernel,
        grid_spec=grid_spec,
        out_shape=[
            jax.ShapeDtypeStruct((rows, cols), F32),
            jax.ShapeDtypeStruct((rows, cols), BF16),
        ],
        compiler_params=params(),
        cost_estimate=pl.CostEstimate(
            flops=4 * rows * blocks * depth * cols,
            bytes_accessed=2 * rows * blocks * depth + 4 * blocks * depth * cols,
            transcendentals=0,
        ),
        name="forward",
    )(pos, mixed, weight, weight)


def gradient_kernel(steps, has_acc, mixed_ref, left_ref, right_ref, *refs):
    if has_acc:
        acc_in, out_ref, acc_ref = refs
    else:
        acc_in = None
        out_ref, acc_ref = refs
    step = pl.program_id(0)
    half = left_ref.shape[1]
    blocks = mixed_ref.shape[0]
    grads = (left_ref[...].astype(F32).T.astype(BF16), right_ref[...].astype(F32).T.astype(BF16))

    def term(b, s):
        return jnp.dot(grads[s], mixed_ref[b], preferred_element_type=F32)

    @pl.when(step == 0)
    def _():
        for b in range(blocks):
            for s in range(2):
                rows = slice(s * half, (s + 1) * half)
                value = term(b, s)
                if has_acc:
                    value = value + acc_in[b, rows, :]
                acc_ref[b, rows, :] = value

    @pl.when(step > 0)
    def _():
        for b in range(blocks):
            for s in range(2):
                rows = slice(s * half, (s + 1) * half)
                acc_ref[b, rows, :] += term(b, s)

    @pl.when(step == steps - 1)
    def _():
        out_ref[...] = acc_ref[...].astype(out_ref.dtype)


def gradient(mixed, left, right, acc, dtype):
    blocks, rows, depth = mixed.shape
    half = left.shape[1]
    tile = min(rows, 256)
    steps = rows // tile
    shape = (blocks, 2 * half, depth)
    whole = pl.BlockSpec(shape, lambda i: (0, 0, 0), pipeline_mode=pl.Buffered(1))
    in_specs = [
        pl.BlockSpec((blocks, tile, depth), lambda i: (0, i, 0)),
        pl.BlockSpec((tile, half), lambda i: (i, 0)),
        pl.BlockSpec((tile, half), lambda i: (i, 0)),
    ]
    operands = [mixed, left, right]
    if acc is not None:
        in_specs.append(whole)
        operands.append(acc)
    return pl.pallas_call(
        functools.partial(gradient_kernel, steps, acc is not None),
        grid=(steps,),
        in_specs=in_specs,
        out_specs=whole,
        out_shape=jax.ShapeDtypeStruct(shape, dtype),
        scratch_shapes=[pltpu.VMEM(shape, F32)],
        compiler_params=params(),
        cost_estimate=pl.CostEstimate(
            flops=4 * rows * blocks * depth * half,
            bytes_accessed=2 * rows * blocks * depth + 4 * blocks * depth * half,
            transcendentals=0,
        ),
        name="gradient",
    )(*operands)


def tensor_sum(value):
    value = value + sum(lax.ppermute(value, "y", ring(4, k)) for k in (1, 2, 3))
    value = value + lax.ppermute(value, "xl", ring(2, 1))
    return value + lax.ppermute(value, "c", ring(2, 1))


def body(states, gain, sharpness, ancestor_ids, proposal, future):
    tokens, width = states.shape
    total_width = gain.shape[0]
    xh, xl = lax.axis_index("xh"), lax.axis_index("xl")
    place = lax.axis_index(("xl", "y", "c"))
    heads = width // HEAD
    out_cols = proposal.shape[1]

    first = lax.ppermute(proposal, ("xh", "xl"), GATHER_A)
    second = lax.ppermute(proposal, ("xh", "xl"), GATHER_B)
    second = jnp.where(xh == xl, proposal, second)
    left_first = xh == 1
    pair = jnp.stack([jnp.where(left_first, first, second), jnp.where(left_first, second, first)])
    weight = lax.all_gather(pair, "z", axis=0, tiled=False)

    wide = states.astype(F32)
    squares = tensor_sum(jnp.sum(wide * wide, axis=1).reshape(-1, GROUP))
    bias = reach_bias(ancestor_ids.reshape(-1, GROUP))
    my_gain = lax.dynamic_slice_in_dim(gain, place * width, width).reshape(1, width)
    my_sharp = lax.dynamic_slice_in_dim(sharpness, place * heads, heads).reshape(1, heads)
    pos = xl.astype(jnp.int32).reshape(1)

    predicted = []
    start = 0
    acc = None
    for index, rows in enumerate(CHUNKS):
        mixed = attention(states, squares, bias, my_gain, my_sharp, total_width, start, rows)
        mixed = lax.all_gather(mixed, ("y", "c"), axis=0, tiled=False)
        keep, send = forward(pos, mixed, weight)
        result = keep + lax.ppermute(send, "xl", ring(2, 1)).astype(F32)
        predicted.append(result.astype(BF16))
        target = lax.slice_in_dim(future, start, start + rows).astype(F32)
        mine = jnp.clip(result - target, -1.0, 1.0).astype(BF16)
        other = lax.ppermute(mine, "xl", ring(2, 1))
        left = jnp.where(xl == 0, mine, other)
        right = jnp.where(xl == 0, other, mine)
        last = index == len(CHUNKS) - 1
        acc = gradient(mixed, left, right, acc, BF16 if last else F32)
        start += rows

    summed = lax.psum_scatter(acc, "z", scatter_dimension=0, tiled=False)
    low, high = summed[:out_cols], summed[out_cols:]
    to_a = jnp.where(xh == 1, low, high)
    to_b = jnp.where(xh == 1, high, low)
    got_a = lax.ppermute(to_a, ("xh", "xl"), SCATTER_A)
    got_b = lax.ppermute(to_b, ("xh", "xl"), SCATTER_B)
    got_b = jnp.where(xh == xl, to_b, got_b)
    weight_grad = (got_a.astype(F32) + got_b.astype(F32)).T / math.sqrt(
        tokens * lax.axis_size("xh") * lax.axis_size("z")
    )
    return jnp.concatenate(predicted), weight_grad


def solution(mesh):
    grid = Mesh(mesh.devices.reshape(2, 8, 2, 4, 2), ("xh", "z", "xl", "y", "c"))
    dp, tensor = ("xh", "z"), ("xl", "y", "c")
    return jax.shard_map(
        body,
        mesh=grid,
        in_specs=(P(dp, tensor), P(), P(), P(dp), P(dp, tensor), P(dp, tensor)),
        out_specs=(P(dp, tensor), P(dp, tensor)),
        check_vma=False,
    )
```

time: 539 us -> 329 us (0.61)
  waiting for transfers between devices: 457 us -> 228 us
  Pallas kernels: 0 us -> 54.5 us
  matrix products: 40.5 us -> 0 us
  starting transfers between devices: 5.99 us -> 23.9 us
  local copies, waits for them, and re-layouts: 14.7 us -> 3.18 us
    reduce_scatter x1, waiting for transfers between devices: 210 us -> 56.4 us  [body(): summed = lax.psum_scatter(acc, 'z', scatter_dimension=0, tiled=False)]
    all_gather x2, waiting for transfers between devices: 219 us -> 109 us  [the longest x1 88 us: body(): mixed = lax.all_gather(mixed, ('y', 'c'), axis=0, tiled=False)]
    ppermute x0 -> x11, waiting for transfers between devices: none -> 62.2 us  [the longest x1 23.9 us: body(): result = keep + lax.ppermute(send, 'xl', ring(2, 1)).astype(F32)]
    pallas_call x0 -> x4, Pallas kernels: none -> 54.5 us  [the longest x1 22.9 us: attention(): pl.pallas_call(functools.partial(attention_kernel, width), grid=(rows //...]
    dot_general x10 -> x0, matrix products: 40.5 us -> none  [the longest x1 17.3 us: body(): lax.dot_general(piece, residual_grad, (((0,), (0,)), ((), ())), preferred...]
    all_to_all x1 -> x0, waiting for transfers between devices: 27.4 us -> none  [body(): lax.all_to_all(final_layer_states, 'tensor', split_axis=0, concat_axis=1,...]
    ppermute x0 -> x11, starting transfers between devices: none -> 23.8 us  [the longest x1 7.06 us: tensor_sum(): value = value + lax.ppermute(value, 'xl', ring(2, 1))]
    convert_element_type x3 -> x0, local copies, waits for them, and re-layouts: 10.5 us -> none  [the longest x2 9.14 us: body(): wide_rows = panel.astype(jnp.float32)]
  transfers between devices with their start and end apart: 4 -> 14, of which waited for: 4 -> 9; matrix products, arithmetic and copies ran while one was open for 5% -> 0% of each run, Pallas kernels for 0% -> 7%
where the time goes in v1:
time: 329 us; the launch traced here: 328 us
  waiting for transfers between devices  228 us (69%)
  Pallas kernels  54.5 us (17%)
  starting transfers between devices  23.9 us (7%)
  between operations  13.9 us (4%)
  other arithmetic  5.11 us (2%)
    all_gather x1, waiting for transfers between devices, body(): mixed = lax.all_gather(mixed, ('y', 'c'), axis=0, tiled=False)  88 us
    reduce_scatter x1, waiting for transfers between devices, body(): summed = lax.psum_scatter(acc, 'z', scatter_dimension=0, tiled=False)  56.4 us
    ppermute x1, waiting for transfers between devices, body(): result = keep + lax.ppermute(send, 'xl', ring(2, 1)).astype(F32)  23.9 us
    ppermute x1, waiting for transfers between devices, body(): other = lax.ppermute(mine, 'xl', ring(2, 1))  23 us
    pallas_call x1, Pallas kernels, attention(): pl.pallas_call(functools.partial(attention_kernel, width), grid=(rows //...  22.9 us
    all_gather x1, waiting for transfers between devices, body(): weight = lax.all_gather(pair, 'z', axis=0, tiled=False)  21 us
    pallas_call x1, Pallas kernels, gradient(): pl.pallas_call(functools.partial(gradient_kernel, steps, acc is not None)...  15.9 us
    pallas_call x1, Pallas kernels, forward(): pl.pallas_call(forward_kernel, grid_spec=grid_spec, out_shape=[jax.ShapeD...  14.3 us
  transfers between devices with their start and end apart: 14, of which 9 were waited for; matrix products, arithmetic and copies ran while one was open for 0% of the time, Pallas kernels for 7%

profile of v1, /device:TPU:8, one launch (start us, length us, event | category | flops | bytes accessed | tf_op | source)
XLA Modules:
  0.0 328.3 jit_solution(1292676420574356545)
XLA Ops:
  7.2 0.0 copy-start
  7.2 0.0 all-gather.7.cloned.1.call-start
  7.2 3.1 collective-permute-start.5
  10.3 0.7 collective-permute-start.6
  11.0 5.2 %collective-permute-done.5 = bf16[512,256]{1,0:T(8,128)(2,1)S(1)} collective-permute-done((bf16[512,256]{1,0:T(8,128)(2,1)}, bf16[512,256]{1,0:T(8,128)(2,1)S(1)}, u32[]{:S(2)}, u32[]{:S(2)}) %collective-permute-start.5) | collective-permute-done | bytes 262176 | tf_op jit(solution)/shard_map/ppermute | solution.py:249
  16.3 0.0 collective-permute-done.6
  16.3 1.0 select_bitcast_fusion.3
  17.3 0.0 copy-start.3
  17.3 0.8 pad_maximum_fusion
  18.1 0.0 all-gather.7.cloned.1.call-update
  18.2 0.0 all-gather.5.cloned.1.call-start
  18.2 0.5 multiply_reduce_fusion
  18.7 1.7 collective-permute-start
  20.4 0.9 collective-permute-start.1
  21.3 2.4 collective-permute-start.2
  23.7 0.0 collective-permute-done
  23.7 1.8 collective-permute-done.1
  25.5 0.0 collective-permute-done.2
  25.5 7.1 %collective-permute-start.3 = (f32[16,128]{1,0:T(8,128)S(1)}, f32[16,128]{1,0:T(8,128)S(1)}, u32[]{:S(2)}, u32[]{:S(2)}) collective-permute-start(f32[16,128]{1,0:T(8,128)S(1)} %add_add_fusion), channel_id=1, source_target_pairs={{0,8},{8,0},{1,9},{9,1},{2,10},{10,2},{3,11},{11,3},{4,12},{12,4},... | collective-permute-start | bytes 24584 | tf_op jit(solution)/shard_map/ppermute | solution.py:237
  32.6 0.1 dynamic-slice_bitcast_fusion.sharp_ref
  32.7 1.6 collective-permute-done.3
  34.2 0.0 collective-permute-start.4
  34.2 1.5 reach.1.bias_ref
  35.7 0.8 dynamic_slice.6
  36.5 0.0 collective-permute-done.4
  36.5 22.9 %attention.1 = bf16[2048,512]{1,0:T(8,128)(2,1)S(1)} custom-call(bf16[2048,512]{1,0:T(8,128)(2,1)S(1)} %copy-done.1, f32[8,2,128]{2,1,0:T(2,128)S(1)} %bitcast.20, f32[2048,128]{1,0:T(8,128)S(1)} %reach.1.bias_ref, f32[1,512]{1,0:T(1,128)S(1)} %bitcast.21, f32[1,4]{1,0:T(1,128)S(1)} %dynamic-slice_bitcast_fusion.sharp_ref), custom_call_target="tpu_custom_call" | custom-call | flops 2147483648 | bytes 4194304 | tf_op jit(solution)/shard_map/attention/pallas_call | solution.py:100
  59.4 1.3 copy-done.2
  60.7 0.0 all-gather.5.cloned.1.call-update
  60.7 0.0 reduce-scatter.2.cloned.1.call-start
  60.8 21.0 %all-gather.7.cloned.1.call-done = bf16[16,512,256]{2,1,0:T(8,128)(2,1)} async-done(((bf16[2,512,256]{2,1,0:T(8,128)(2,1)}), bf16[16,512,256]{2,1,0:T(8,128)(2,1)}) %all-gather.7.cloned.1.call-update) | async-done | bytes 4194320 | tf_op jit(solution)/shard_map/all_gather | solution.py:254
  81.7 88.0 %all-gather.5.cloned.1.call-done = bf16[16384,512]{1,0:T(8,128)(2,1)} async-done(((bf16[2048,512]{1,0:T(8,128)(2,1)}), bf16[16384,512]{1,0:T(8,128)(2,1)}) %all-gather.5.cloned.1.call-update) | async-done | bytes 16777232 | tf_op jit(solution)/shard_map/all_gather | solution.py:268
  169.7 14.3 %forward.1 = (f32[2048,256]{1,0:T(8,128)S(1)}, bf16[2048,256]{1,0:T(8,128)(2,1)S(1)}) custom-call(s32[1]{0:T(128)} %bitcast.pos_ref, bf16[8,2048,512]{2,1,0:T(8,128)(2,1)} %bitcast.26, bf16[8,2,512,256]{3,2,1,0:T(8,128)(2,1)} %bitcast.28, bf16[8,2,512,256]{3,2,1,0:T(8,128)(2,1)} %bitcast.29), custom_call_target="tpu_custom_call" | custom-call | flops 8589934592 | bytes 20971520 | tf_op jit(solution)/shard_map/forward/pallas_call | solution.py:149
  184.0 1.6 collective-permute-start.7
  185.6 23.9 %collective-permute-done.7 = bf16[2048,256]{1,0:T(8,128)(2,1)S(1)} collective-permute-done((bf16[2048,256]{1,0:T(8,128)(2,1)S(1)}, bf16[2048,256]{1,0:T(8,128)(2,1)S(1)}, u32[]{:S(2)}, u32[]{:S(2)}) %collective-permute-start.7) | collective-permute-done | bytes 1048608 | tf_op jit(solution)/shard_map/ppermute | solution.py:270
  209.4 1.4 clamp_convert_fusion
  210.9 1.5 collective-permute-start.8
  212.4 23.0 %collective-permute-done.8 = bf16[2048,256]{1,0:T(8,128)(2,1)S(1)} collective-permute-done((bf16[2048,256]{1,0:T(8,128)(2,1)S(1)}, bf16[2048,256]{1,0:T(8,128)(2,1)S(1)}, u32[]{:S(2)}, u32[]{:S(2)}) %collective-permute-start.8) | collective-permute-done | bytes 1048608 | tf_op jit(solution)/shard_map/ppermute | solution.py:274
  235.4 0.1 broadcast_select_fusion
  235.6 15.9 %gradient.1 = bf16[8,512,512]{2,1,0:T(8,128)(2,1)} custom-call(bf16[8,2048,512]{2,1,0:T(8,128)(2,1)} %bitcast.27, bf16[2048,256]{1,0:T(8,128)(2,1)S(1)} %get-tuple-element.13.left_ref, bf16[2048,256]{1,0:T(8,128)(2,1)S(1)} %get-tuple-element.12.right_ref), custom_call_target="tpu_custom_call" | custom-call | flops 8589934592 | bytes 20971520 | tf_op jit(solution)/shard_map/gradient/pallas_call | solution.py:218
  251.5 0.0 reduce-scatter.2.cloned.1.call-update
  251.5 56.4 %reduce-scatter.2.cloned.1.call-done = bf16[1,512,512]{2,1,0:T(8,128)(2,1)} async-done(((bf16[8,512,512]{2,1,0:T(8,128)(2,1)}), bf16[1,512,512]{2,1,0:T(8,128)(2,1)}) %reduce-scatter.2.cloned.1.call-update) | async-done | bytes 524304 | tf_op jit(solution)/shard_map/reduce_scatter | solution.py:281
  307.9 1.1 select_bitcast_fusion
  309.0 0.7 collective-permute-start.10
  309.7 4.2 %collective-permute-start.9 = (bf16[256,512]{1,0:T(8,128)(2,1)S(1)}, bf16[256,512]{1,0:T(8,128)(2,1)S(1)}, u32[]{:S(2)}, u32[]{:S(2)}) collective-permute-start(bf16[256,512]{1,0:T(8,128)(2,1)S(1)} %get-tuple-element.17), channel_id=1, source_target_pairs={{128,0},{0,8},{136,128},{8,136},{129,1},{1,9},{137,129},{9,137},{1... | collective-permute-start | bytes 786440 | tf_op jit(solution)/shard_map/ppermute | solution.py:285
  313.9 0.0 collective-permute-done.10
  313.9 6.7 %collective-permute-done.9 = bf16[256,512]{1,0:T(8,128)(2,1)S(1)} collective-permute-done((bf16[256,512]{1,0:T(8,128)(2,1)S(1)}, bf16[256,512]{1,0:T(8,128)(2,1)S(1)}, u32[]{:S(2)}, u32[]{:S(2)}) %collective-permute-start.9) | collective-permute-done | bytes 262176 | tf_op jit(solution)/shard_map/ppermute | solution.py:285
  320.6 0.1 multiply_bitcast_fusion
  320.7 1.0 copy.9
  (10 shorter events, 0.0 us)
Async XLA Ops:
  7.2 25.4 %copy-start = (f32[64]{0:T(128)S(1)}, f32[64]{0:T(128)}, u32[]{:S(2)}) copy-start(f32[64]{0:T(128)} %param.8) | copy-start | bytes 772
  7.2 11.0 %copy-start.1 = (bf16[2048,512]{1,0:T(8,128)(2,1)S(1)}, bf16[2048,512]{1,0:T(8,128)(2,1)}, u32[]{:S(2)}) copy-start(bf16[2048,512]{1,0:T(8,128)(2,1)} %x_ref.1) | copy-start | bytes 6291460
  7.2 74.5 %all-gather.7.cloned.1.call-start = ((), (), s32[]{:S(2)}) async-start(), calls=%async_computation.3 | async-start | bytes 4718592 | tf_op jit(solution)/shard_map/all_gather | solution.py:254
  7.2 9.0 %collective-permute-start.5 = (bf16[512,256]{1,0:T(8,128)(2,1)}, bf16[512,256]{1,0:T(8,128)(2,1)S(1)}, u32[]{:S(2)}, u32[]{:S(2)}) collective-permute-start(bf16[512,256]{1,0:T(8,128)(2,1)} %param.10), channel_id=1, source_target_pairs={{0,128},{8,0},{128,136},{136,8},{1,129},{9,1},{129,137},{137,9},{2... | collective-permute-start | bytes 786440 | tf_op jit(solution)/shard_map/ppermute | solution.py:249
  10.3 5.9 %collective-permute-start.6 = (bf16[512,256]{1,0:T(8,128)(2,1)}, bf16[512,256]{1,0:T(8,128)(2,1)S(1)}, u32[]{:S(2)}, u32[]{:S(2)}) collective-permute-start(bf16[512,256]{1,0:T(8,128)(2,1)} %param.10), channel_id=1, source_target_pairs={{8,128},{128,8},{9,129},{129,9},{10,130},{130,10},{11,131},{131,11... | collective-permute-start | bytes 786440 | tf_op jit(solution)/shard_map/ppermute | solution.py:250
  17.3 16.9 %copy-start.3 = (s32[2048]{0:T(1024)S(1)}, s32[2048]{0:T(1024)}, u32[]{:S(2)}) copy-start(s32[2048]{0:T(1024)} %param.9) | copy-start | bytes 24580
  18.2 151.6 %all-gather.5.cloned.1.call-start = ((), (), s32[]{:S(2)}) async-start(), calls=%async_computation.2 | async-start | bytes 18874368 | tf_op jit(solution)/shard_map/all_gather | solution.py:268
  18.7 5.0 %collective-permute-start = (f32[16,128]{1,0:T(8,128)S(1)}, f32[16,128]{1,0:T(8,128)S(1)}, u32[]{:S(2)}, u32[]{:S(2)}) collective-permute-start(f32[16,128]{1,0:T(8,128)S(1)} %bitcast.23), channel_id=1, source_target_pairs={{0,2},{2,4},{4,6},{6,0},{1,3},{3,5},{5,7},{7,1},{8,10},{10,12},{12... | collective-permute-start | bytes 24584 | tf_op jit(solution)/shard_map/ppermute | solution.py:236
  20.4 5.2 %collective-permute-start.1 = (f32[16,128]{1,0:T(8,128)S(1)}, f32[16,128]{1,0:T(8,128)S(1)}, u32[]{:S(2)}, u32[]{:S(2)}) collective-permute-start(f32[16,128]{1,0:T(8,128)S(1)} %bitcast.24), channel_id=1, source_target_pairs={{0,4},{2,6},{4,0},{6,2},{1,5},{3,7},{5,1},{7,3},{8,12},{10,14},{12... | collective-permute-start | bytes 24584 | tf_op jit(solution)/shard_map/ppermute | solution.py:236
  21.3 4.2 %collective-permute-start.2 = (f32[16,128]{1,0:T(8,128)S(1)}, f32[16,128]{1,0:T(8,128)S(1)}, u32[]{:S(2)}, u32[]{:S(2)}) collective-permute-start(f32[16,128]{1,0:T(8,128)S(1)} %bitcast.25), channel_id=1, source_target_pairs={{0,6},{2,0},{4,2},{6,4},{1,7},{3,1},{5,3},{7,5},{8,14},{10,8},{12,... | collective-permute-start | bytes 24584 | tf_op jit(solution)/shard_map/ppermute | solution.py:236
  25.5 8.7 %collective-permute-start.3 = (f32[16,128]{1,0:T(8,128)S(1)}, f32[16,128]{1,0:T(8,128)S(1)}, u32[]{:S(2)}, u32[]{:S(2)}) collective-permute-start(f32[16,128]{1,0:T(8,128)S(1)} %add_add_fusion), channel_id=1, source_target_pairs={{0,8},{8,0},{1,9},{9,1},{2,10},{10,2},{3,11},{11,3},{4,12},{12,4},... | collective-permute-start | bytes 24584 | tf_op jit(solution)/shard_map/ppermute | solution.py:237
  34.2 2.3 collective-permute-start.4
  59.3 1.3 copy-start.2
  60.7 247.2 %reduce-scatter.2.cloned.1.call-start = ((), (), s32[]{:S(2)}) async-start(), calls=%async_computation.1 | async-start | bytes 4718592 | tf_op jit(solution)/shard_map/reduce_scatter | solution.py:281
  169.7 39.7 %copy-start.4 = (bf16[2048,256]{1,0:T(8,128)(2,1)S(1)}, bf16[2048,256]{1,0:T(8,128)(2,1)}, u32[]{:S(2)}) copy-start(bf16[2048,256]{1,0:T(8,128)(2,1)} %param.11) | copy-start | bytes 3145732
  184.0 25.4 %collective-permute-start.7 = (bf16[2048,256]{1,0:T(8,128)(2,1)S(1)}, bf16[2048,256]{1,0:T(8,128)(2,1)S(1)}, u32[]{:S(2)}, u32[]{:S(2)}) collective-permute-start(bf16[2048,256]{1,0:T(8,128)(2,1)S(1)} %get-tuple-element.5), channel_id=1, source_target_pairs={{0,8},{8,0},{1,9},{9,1},{2,10},{10,2},{3,11},{11,3},{4,12},{12,4},... | collective-permute-start | bytes 3145736 | tf_op jit(solution)/shard_map/ppermute | solution.py:270
  210.9 24.5 %collective-permute-start.8 = (bf16[2048,256]{1,0:T(8,128)(2,1)S(1)}, bf16[2048,256]{1,0:T(8,128)(2,1)S(1)}, u32[]{:S(2)}, u32[]{:S(2)}) collective-permute-start(bf16[2048,256]{1,0:T(8,128)(2,1)S(1)} %get-tuple-element.10), channel_id=1, source_target_pairs={{0,8},{8,0},{1,9},{9,1},{2,10},{10,2},{3,11},{11,3},{4,12},{12,4},... | collective-permute-start | bytes 3145736 | tf_op jit(solution)/shard_map/ppermute | solution.py:274
  309.0 4.9 %collective-permute-start.10 = (bf16[256,512]{1,0:T(8,128)(2,1)S(1)}, bf16[256,512]{1,0:T(8,128)(2,1)S(1)}, u32[]{:S(2)}, u32[]{:S(2)}) collective-permute-start(bf16[256,512]{1,0:T(8,128)(2,1)S(1)} %get-tuple-element.16), channel_id=1, source_target_pairs={{8,128},{128,8},{9,129},{129,9},{10,130},{130,10},{11,131},{131,11... | collective-permute-start | bytes 786440 | tf_op jit(solution)/shard_map/ppermute | solution.py:286
  309.7 10.9 %collective-permute-start.9 = (bf16[256,512]{1,0:T(8,128)(2,1)S(1)}, bf16[256,512]{1,0:T(8,128)(2,1)S(1)}, u32[]{:S(2)}, u32[]{:S(2)}) collective-permute-start(bf16[256,512]{1,0:T(8,128)(2,1)S(1)} %get-tuple-element.17), channel_id=1, source_target_pairs={{128,0},{0,8},{136,128},{8,136},{129,1},{1,9},{137,129},{9,137},{1... | collective-permute-start | bytes 786440 | tf_op jit(solution)/shard_map/ppermute | solution.py:285
Sparse Core Ops, SparseCore 0:
  18.3 63.3 all-gather.6
  83.6 86.1 all-gather.4
  251.6 56.2 reduce-scatter.1
